TPU v7x, 32 devices: a whole 2x2x4 slice. The times are simulated.
32 devices in a mesh: groups: 1, ep: 16 (over z, y, x), sub: 2 (over core).
Axes of the slice: x: 2, y: 2, z: 4, core: 2. Of those that a mesh axis runs over, the one named last changes fastest.
Arguments:
- expert_inputs: bfloat16 [2, 512, 8, 768], P(None, ('groups', 'ep', 'sub')), may hold values from -6 to 6
- routes: int32 [2, 512, 8], P(None, ('groups', 'ep', 'sub')), may hold values from 0 to 15, all different within a row; in each aligned block of 16 rows (0 to 15, 16 to 31, ..., all dimensions but the last counted through in order) at most 16 rows name the same one
- route_weights: float32 [2, 512, 8], P(None, ('groups', 'ep', 'sub')), may hold values from 0.05 to 0.5
- master: float32 [16, 768, 2048], P('ep', 'sub'), as said below
- old_steps: float32 [16, 6, 2048], P('ep', 'sub'), as said below
- move_list: int32 [16, 4], replicated, may hold values from 0 to 15, as said below
Outputs:
- mixed: bfloat16 [2, 512, 2048], P(None, ('groups', 'ep', 'sub'))
- new_levels: bfloat16 [16, 768, 2048], P(('groups', 'ep'), 'sub')
- new_steps: float32 [16, 6, 2048], P(('groups', 'ep'), 'sub')
Inputs may be any that keep to these rules, and one draw needn't show every extreme that they name: `routes`: in each step the 8 experts of a token differ, and in each aligned block of 16 tokens, the tokens of one device, no expert is named by more than 16 of them; some expert is named by exactly 16. `move_list`: every expert has one row; the old owners, and the new owners, each take every index of ep once; no expert keeps its owner; the expert that arrives at a device moves in the same step as the one that leaves it. `master`: in every block of 128 rows of one column, one entry has the largest magnitude m, and every entry lies within 0.3 m / 127 of a whole multiple of m / 127. `old_steps`: Positive.
All inputs are finite; a program needn't handle non-finite values.
Results may differ from a plain program's by a relative error of at most 0.0059.
Values may be sent and summed in bfloat16 or wider, within the bound.
A program may use at most 64 MiB of HBM per device.

v0:
```python
import jax
import jax.numpy as jnp
from jax import lax
from jax.sharding import PartitionSpec as P

Q_BLOCK = 128


EPSILON = 1e-06


def grid_of(weights):
    blocks = weights.reshape(-1, Q_BLOCK, weights.shape[-1])
    return (jnp.max(jnp.abs(blocks), axis=1) + EPSILON) / 127.0


def levels_of(weights, step_grid):
    blocks = weights.reshape(step_grid.shape[0], Q_BLOCK, weights.shape[-1])
    nearest = jnp.floor(blocks / step_grid[:, None, :] + 0.5)
    return jnp.clip(nearest, -127.0, 127.0).reshape(weights.shape).astype(jnp.bfloat16)


def dequantize(levels, step_grid):
    blocks = levels.reshape(step_grid.shape[0], Q_BLOCK, levels.shape[-1]).astype(jnp.float32)
    return (blocks * step_grid[:, None, :]).reshape(levels.shape)


def lookup(key_column, value_column, queries):
    matches = key_column[None, :] == queries[:, None]
    return jnp.sum(jnp.where(matches, value_column[None, :], 0), axis=1)


def local(expert_inputs, routes, route_weights, master, old_steps, move_list):
    experts = lax.axis_size("ep")
    my_index = lax.axis_index("ep")
    step_count, token_count, top_count, inner_width = expert_inputs.shape
    half_width = master.shape[1]
    out_width = master.shape[2]
    capacity = min(token_count, max(2, 2 * token_count * top_count // experts))
    all_experts = jnp.arange(experts, dtype=jnp.int32)
    expert_column = move_list[:, 0]
    old_column = move_list[:, 1]
    new_column = move_list[:, 2]
    step_column = move_list[:, 3]
    old_owner = lookup(expert_column, old_column, all_experts)
    new_owner = lookup(expert_column, new_column, all_experts)
    move_step = lookup(expert_column, step_column, all_experts)
    arrive_from = lookup(new_column, old_column, all_experts)
    leave_step = lookup(old_column, step_column, jnp.reshape(my_index, (1,)))[0]
    own_master = master[0]
    stale_grid = old_steps[0]
    stale_levels = levels_of(own_master, stale_grid)
    spread = lax.all_to_all(
        own_master.reshape(experts, -1), "ep", split_axis=0, concat_axis=0, tiled=True
    )
    arrived = lax.all_to_all(
        spread[arrive_from], "ep", split_axis=0, concat_axis=0, tiled=True
    ).reshape(half_width, out_width)
    new_grid = grid_of(arrived)
    new_levels = levels_of(arrived, new_grid)
    both_weights = jnp.stack(
        [dequantize(stale_levels, stale_grid), dequantize(new_levels, new_grid)]
    )
    slot_numbers = jnp.arange(experts * capacity, dtype=jnp.int32)
    results = []
    for step_index in range(step_count):
        active = (step_index >= leave_step).astype(jnp.int32)
        weights_now = lax.dynamic_index_in_dim(both_weights, active, 0, keepdims=False)
        target_owner = jnp.where(move_step <= step_index, new_owner, old_owner)
        expert_ids = routes[step_index].reshape(-1)
        token_rows = expert_inputs[step_index].reshape(-1, inner_width)
        matches = expert_ids[:, None] == all_experts[None, :]
        hit_counts = matches.astype(jnp.int32)
        before = jnp.cumsum(hit_counts, axis=0) - hit_counts
        slot_rank = jnp.sum(jnp.where(matches, before, 0), axis=1)
        target_device = jnp.sum(jnp.where(matches, target_owner[None, :], 0), axis=1)
        selector = (target_device * capacity + slot_rank)[:, None] == slot_numbers[None, :]
        outgoing = jnp.dot(
            jnp.transpose(selector).astype(jnp.bfloat16),
            token_rows,
            preferred_element_type=jnp.float32,
        ).astype(jnp.bfloat16)
        outgoing = outgoing.reshape(experts, capacity, 2, half_width)
        arriving = lax.all_to_all(
            lax.all_to_all(outgoing, "ep", split_axis=0, concat_axis=0, tiled=True),
            "sub",
            split_axis=2,
            concat_axis=2,
            tiled=True,
        )
        arriving_rows = arriving.reshape(-1, half_width).astype(jnp.float32)
        running = jnp.dot(arriving_rows, weights_now, precision=lax.Precision.HIGHEST)
        partial_value = running.astype(jnp.bfloat16).reshape(experts, capacity, 2, out_width)
        joined = lax.all_to_all(partial_value, "sub", split_axis=2, concat_axis=2, tiled=True)
        summed = (joined[:, :, 0].astype(jnp.float32) + joined[:, :, 1].astype(jnp.float32)).astype(
            jnp.bfloat16
        )
        returned = lax.all_to_all(summed, "ep", split_axis=0, concat_axis=0, tiled=True)
        weighted = jnp.where(selector, route_weights[step_index].reshape(-1)[:, None], 0.0)
        mixing = jnp.sum(weighted.reshape(token_count, top_count, -1), axis=1)
        combined = jnp.dot(
            mixing,
            returned.reshape(-1, out_width).astype(jnp.float32),
            precision=lax.Precision.HIGHEST,
        )
        results.append(combined.astype(jnp.bfloat16))
    level_output = (new_levels.astype(jnp.float32) * 0.0078125).astype(jnp.bfloat16)[None]
    return (jnp.stack(results), level_output, new_grid[None])


def solution(mesh):
    placed = (
        P(None, ("groups", "ep", "sub"), None, None),
        P(None, ("groups", "ep", "sub"), None),
        P(None, ("groups", "ep", "sub"), None),
        P("ep", "sub", None),
        P("ep", "sub", None),
        P(),
    )
    return jax.shard_map(
        local,
        mesh=mesh,
        in_specs=placed,
        out_specs=(
            P(None, ("groups", "ep", "sub"), None),
            P(("groups", "ep"), "sub", None),
            P(("groups", "ep"), "sub", None),
        ),
        check_vma=False,
    )
```

profile of v0, /device:TPU:0, one launch (start us, length us, event | category | flops | bytes accessed | tf_op | source)
XLA Modules:
  0.0 355.1 jit_solution(15753400084253739029)
XLA Ops:
  0.6 0.7 fusion.43
  1.9 0.2 reduce_window_sum.17
  2.0 0.2 reduce_window_sum.18
  2.2 1.5 fusion.37
  3.8 0.6 select_reduce_fusion.6
  4.4 0.2 select_reduce_fusion.3
  4.6 2.0 convolution_convert_fusion.3
  6.7 1.1 reshape.262
  7.8 0.8 copy.54
  8.5 8.3 %all-to-all-start = ((bf16[16,16,2,384]{3,1,2,0:T(8,128)(2,1)}), bf16[16,16,2,384]{3,1,2,0:T(8,128)(2,1)S(1)}, u32[]{:S(2)}, u32[]{:S(2)}) async-start(bf16[16,16,2,384]{3,1,2,0:T(8,128)(2,1)} %copy.54), calls=%async_computation | async-start | bytes 786432 | tf_op jit(solution)/shard_map/all_to_all | solution.py:85
  16.9 2.0 convolution_convert_fusion.2
  18.9 1.8 reshape.266
  20.8 1.8 copy.61
  22.5 7.0 %all-to-all-done = bf16[16,16,2,384]{3,1,2,0:T(8,128)(2,1)S(1)} async-done(((bf16[16,16,2,384]{3,1,2,0:T(8,128)(2,1)}), bf16[16,16,2,384]{3,1,2,0:T(8,128)(2,1)S(1)}, u32[]{:S(2)}, u32[]{:S(2)}) %all-to-all-start) | async-done | bytes 393248 | tf_op jit(solution)/shard_map/all_to_all | solution.py:85
  29.5 4.2 %all-to-all-start.6 = ((bf16[16,16,2,384]{3,1,2,0:T(8,128)(2,1)}), bf16[16,16,2,384]{3,1,2,0:T(8,128)(2,1)}, u32[]{:S(2)}, u32[]{:S(2)}) async-start(bf16[16,16,2,384]{3,1,2,0:T(8,128)(2,1)} %copy.61), calls=%async_computation.6 | async-start | bytes 786432 | tf_op jit(solution)/shard_map/all_to_all | solution.py:85
  33.7 4.7 %all_to_all.40 = f32[16,1,49152]{2,1,0:T(1,128)} reshape(f32[1,384,2048]{2,1,0:T(8,128)S(1)} %copy-done.2) | data formatting | bytes 6291456 | tf_op jit(solution)/shard_map/all_to_all | solution.py:53
  38.4 6.8 %all-to-all-done.6 = bf16[16,16,2,384]{3,1,2,0:T(8,128)(2,1)} async-done(((bf16[16,16,2,384]{3,1,2,0:T(8,128)(2,1)}), bf16[16,16,2,384]{3,1,2,0:T(8,128)(2,1)}, u32[]{:S(2)}, u32[]{:S(2)}) %all-to-all-start.6) | async-done | bytes 393248 | tf_op jit(solution)/shard_map/all_to_all | solution.py:85
  45.2 3.7 %all-to-all-start.2 = ((f32[16,1,49152]{2,1,0:T(1,128)}), f32[16,1,49152]{2,1,0:T(1,128)S(1)}, u32[]{:S(2)}, u32[]{:S(2)}) async-start(f32[16,1,49152]{2,1,0:T(1,128)} %all_to_all.40), calls=%async_computation.2 | async-start | bytes 6291456 | tf_op jit(solution)/shard_map/all_to_all | solution.py:53
  49.0 0.8 copy.55
  49.8 1.8 copy.62
  51.6 57.6 %all-to-all-done.2 = f32[16,1,49152]{2,1,0:T(1,128)S(1)} async-done(((f32[16,1,49152]{2,1,0:T(1,128)}), f32[16,1,49152]{2,1,0:T(1,128)S(1)}, u32[]{:S(2)}, u32[]{:S(2)}) %all-to-all-start.2) | async-done | bytes 3145760 | tf_op jit(solution)/shard_map/all_to_all | solution.py:53
  109.2 1.7 copy-done.1
  110.9 3.5 all-to-all-start.1
  114.4 3.7 %copy.69 = f32[16,1,49152]{2,0,1:T(8,128)S(1)} copy(f32[16,1,49152]{2,1,0:T(1,128)} %copy-done.1) | data formatting | bytes 6291456
  118.1 3.1 gather_fusion
  121.1 6.8 %copy.57 = f32[16,1,49152]{2,1,0:T(1,128)} copy(f32[16,1,49152]{2,0,1:T(8,128)} %bitcast.86) | data formatting | bytes 6291456 | tf_op jit(solution)/shard_map/all_to_all | solution.py:56
  128.0 4.8 %all_to_all.61 = bf16[16,16,2,384]{3,1,0,2:T(8,128)(2,1)} all-to-all(bf16[16,16,2,384]{3,1,0,2:T(8,128)(2,1)S(1)} %copy-done.5), channel_id=1, replica_groups=mesh['groups'=1,'ep'=16,'sub'=2] {'sub'}, dimensions={2} | all-to-all | bytes 786432 | tf_op jit(solution)/shard_map/all_to_all | solution.py:84
  132.8 14.2 %all-to-all-start.3 = ((f32[16,1,49152]{2,1,0:T(1,128)}), f32[16,1,49152]{2,1,0:T(1,128)}, u32[]{:S(2)}, u32[]{:S(2)}) async-start(f32[16,1,49152]{2,1,0:T(1,128)} %copy.57), calls=%async_computation.3 | async-start | bytes 6291456 | tf_op jit(solution)/shard_map/all_to_all | solution.py:56
  148.3 0.4 div.47
  148.7 2.7 bitcast_multiply_fusion.1
  151.4 1.2 copy.56
  152.5 1.9 reshape.263
  154.4 2.1 copy.63
  156.6 1.1 reshape.267
  157.7 50.5 %all-to-all-done.3 = f32[16,1,49152]{2,1,0:T(1,128)} async-done(((f32[16,1,49152]{2,1,0:T(1,128)}), f32[16,1,49152]{2,1,0:T(1,128)}, u32[]{:S(2)}, u32[]{:S(2)}) %all-to-all-start.3) | async-done | bytes 3145760 | tf_op jit(solution)/shard_map/all_to_all | solution.py:56
  208.2 20.1 %fusion.41 = (f32[16,49152]{1,0:T(8,128)}, f32[16,49152]{1,0:T(8,128)}) fusion(f32[16,1,49152]{2,1,0:T(1,128)} %all-to-all-done.3), kind=kLoop, calls=%fused_computation.87 | loop fusion | flops 786432 | bytes 9437184 | tf_op jit(solution)/shard_map/all_to_all | solution.py:56
  228.3 3.4 abs.7
  231.7 2.7 reduce_max.9
  234.4 1.4 add_multiply_fusion
  235.8 3.4 reshape_reshape.4
  239.2 1.3 div.52
  240.5 0.6 copy-done.3
  241.1 2.0 fusion
  243.1 0.4 bitcast_multiply_fusion
  243.6 1.7 copy-done
  245.2 4.9 %fusion.17 = bf16[512,2048]{1,0:T(8,128)(2,1)} fusion(bf16[512,384]{1,0:T(8,128)(2,1)S(1)} %copy-done.4, s32[]{:T(128)S(6)} %select_n.91, f32[1,384,2048]{2,1,0:T(8,128)S(1)} %bitcast_multiply_fusion.1, f32[1,384,2048]{2,1,0:T(8,128)S(1)} %bitcast_multiply_fusion), kind=kOutput, calls=%fused_computation.27 | convolution fusion | flops 4833673216 | bytes 8781828 | tf_op jit(solution)/shard_map/dot_general | solution.py:92
  250.1 4.4 %reshape.264 = bf16[16,16,2,2048]{3,2,1,0:T(2,128)(2,1)} reshape(bf16[512,2048]{1,0:T(8,128)(2,1)} %fusion.17) | data formatting | bytes 4194304 | tf_op jit(solution)/shard_map/reshape | solution.py:93
  254.5 3.8 %copy.58 = bf16[16,16,2,2048]{3,1,0,2:T(8,128)(2,1)} copy(bf16[16,16,2,2048]{3,2,1,0:T(2,128)(2,1)} %reshape.264) | data formatting | bytes 4194304 | tf_op jit(solution)/shard_map/reshape | solution.py:93
  258.4 5.0 %all-to-all-start.4 = ((bf16[16,16,2,2048]{3,1,0,2:T(8,128)(2,1)}), bf16[16,16,2,2048]{3,1,0,2:T(8,128)(2,1)}, u32[]{:S(2)}, u32[]{:S(2)}) async-start(bf16[16,16,2,2048]{3,1,0,2:T(8,128)(2,1)} %copy.58), calls=%async_computation.4 | async-start | bytes 4194304 | tf_op jit(solution)/shard_map/all_to_all | solution.py:94
  263.4 7.6 %fusion.20 = bf16[512,2048]{1,0:T(8,128)(2,1)} fusion(bf16[512,384]{1,0:T(8,128)(2,1)S(1)} %reshape.267, s32[]{:T(128)S(6)} %select_n.96, f32[1,384,2048]{2,1,0:T(8,128)S(1)} %bitcast_multiply_fusion.1, f32[1,384,2048]{2,1,0:T(8,128)} %copy-done), kind=kOutput, calls=%fused_computation.28 | convolution fusion | flops 4833673216 | bytes 8781828 | tf_op jit(solution)/shard_map/dot_general | solution.py:92
  271.0 3.2 reshape.268
  274.1 2.2 copy.64
  276.4 3.8 %all-to-all-start.8 = ((bf16[16,16,2,2048]{3,1,0,2:T(8,128)(2,1)}), bf16[16,16,2,2048]{3,1,0,2:T(8,128)(2,1)S(1)}, u32[]{:S(2)}, u32[]{:S(2)}) async-start(bf16[16,16,2,2048]{3,1,0,2:T(8,128)(2,1)} %copy.64), calls=%async_computation.8 | async-start | bytes 4194304 | tf_op jit(solution)/shard_map/all_to_all | solution.py:94
  280.1 2.9 fusion.25
  283.1 15.5 %all-to-all-start.5 = ((bf16[16,16,2048]{2,1,0:T(8,128)(2,1)}), bf16[16,16,2048]{2,1,0:T(8,128)(2,1)S(1)}, u32[]{:S(2)}, u32[]{:S(2)}) async-start(bf16[16,16,2048]{2,1,0:T(8,128)(2,1)} %fusion.25), calls=%async_computation.5 | async-start | bytes 2097152 | tf_op jit(solution)/shard_map/all_to_all | solution.py:98
  298.6 1.4 fusion.26
  300.0 23.4 %all-to-all-done.5 = bf16[16,16,2048]{2,1,0:T(8,128)(2,1)S(1)} async-done(((bf16[16,16,2048]{2,1,0:T(8,128)(2,1)}), bf16[16,16,2048]{2,1,0:T(8,128)(2,1)S(1)}, u32[]{:S(2)}, u32[]{:S(2)}) %all-to-all-start.5) | async-done | bytes 1048608 | tf_op jit(solution)/shard_map/all_to_all | solution.py:98
  323.4 6.8 %all-to-all-start.9 = ((bf16[16,16,2048]{2,1,0:T(8,128)(2,1)}), bf16[16,16,2048]{2,1,0:T(8,128)(2,1)S(1)}, u32[]{:S(2)}, u32[]{:S(2)}) async-start(bf16[16,16,2048]{2,1,0:T(8,128)(2,1)} %fusion.26), calls=%async_computation.9 | async-start | bytes 2097152 | tf_op jit(solution)/shard_map/all_to_all | solution.py:98
  330.6 0.1 select_reduce_fusion
  330.8 0.6 div.55
  331.4 0.5 fusion.23
  331.9 22.0 %all-to-all-done.9 = bf16[16,16,2048]{2,1,0:T(8,128)(2,1)S(1)} async-done(((bf16[16,16,2048]{2,1,0:T(8,128)(2,1)}), bf16[16,16,2048]{2,1,0:T(8,128)(2,1)S(1)}, u32[]{:S(2)}, u32[]{:S(2)}) %all-to-all-start.9) | async-done | bytes 1048608 | tf_op jit(solution)/shard_map/all_to_all | solution.py:98
  353.9 0.5 fusion.24
  354.4 0.7 pad_maximum_fusion
  (38 shorter events, 1.0 us)
Async XLA Ops:
  1.9 31.9 %copy-start.2 = (f32[1,384,2048]{2,1,0:T(8,128)S(1)}, f32[1,384,2048]{2,1,0:T(8,128)}, u32[]{:S(2)}) copy-start(f32[1,384,2048]{2,1,0:T(8,128)} %param.9) | copy-start | bytes 9437188
  8.5 21.0 %all-to-all-start = ((bf16[16,16,2,384]{3,1,2,0:T(8,128)(2,1)}), bf16[16,16,2,384]{3,1,2,0:T(8,128)(2,1)S(1)}, u32[]{:S(2)}, u32[]{:S(2)}) async-start(bf16[16,16,2,384]{3,1,2,0:T(8,128)(2,1)} %copy.54), calls=%async_computation | async-start | bytes 786432 | tf_op jit(solution)/shard_map/all_to_all | solution.py:85
  29.5 15.7 %all-to-all-start.6 = ((bf16[16,16,2,384]{3,1,2,0:T(8,128)(2,1)}), bf16[16,16,2,384]{3,1,2,0:T(8,128)(2,1)}, u32[]{:S(2)}, u32[]{:S(2)}) async-start(bf16[16,16,2,384]{3,1,2,0:T(8,128)(2,1)} %copy.61), calls=%async_computation.6 | async-start | bytes 786432 | tf_op jit(solution)/shard_map/all_to_all | solution.py:85
  38.4 10.5 %copy-start.9 = (s32[16]{0:T(128)S(1)}, s32[16]{0:T(128)}, u32[]{:S(2)}) copy-start(s32[16]{0:T(128)} %get-tuple-element.7) | copy-start | bytes 196
  45.2 64.0 %all-to-all-start.2 = ((f32[16,1,49152]{2,1,0:T(1,128)}), f32[16,1,49152]{2,1,0:T(1,128)S(1)}, u32[]{:S(2)}, u32[]{:S(2)}) async-start(f32[16,1,49152]{2,1,0:T(1,128)} %all_to_all.40), calls=%async_computation.2 | async-start | bytes 6291456 | tf_op jit(solution)/shard_map/all_to_all | solution.py:53
  109.2 1.7 copy-start.1
  110.9 17.1 %all-to-all-start.1 = ((bf16[16,16,2,384]{3,1,0,2:T(8,128)(2,1)}), bf16[16,16,2,384]{3,1,0,2:T(8,128)(2,1)S(1)}, u32[]{:S(2)}, u32[]{:S(2)}) async-start(bf16[16,16,2,384]{3,1,0,2:T(8,128)(2,1)} %copy.55), calls=%async_computation.1 | async-start | bytes 786432 | tf_op jit(solution)/shard_map/all_to_all | solution.py:84
  121.1 6.8 %copy-start.5 = (bf16[16,16,2,384]{3,1,0,2:T(8,128)(2,1)S(1)}, bf16[16,16,2,384]{3,1,0,2:T(8,128)(2,1)}, u32[]{:S(2)}) copy-start(bf16[16,16,2,384]{3,1,0,2:T(8,128)(2,1)} %copy.62) | copy-start | bytes 1179652
  132.8 15.5 %copy-start.7 = (f32[1,3,2048]{2,0,1:T(1,128)S(1)}, f32[1,3,2048]{2,0,1:T(1,128)}, u32[]{:S(2)}) copy-start(f32[1,3,2048]{2,0,1:T(1,128)} %param.10) | copy-start | bytes 73732
  132.8 75.5 %all-to-all-start.3 = ((f32[16,1,49152]{2,1,0:T(1,128)}), f32[16,1,49152]{2,1,0:T(1,128)}, u32[]{:S(2)}, u32[]{:S(2)}) async-start(f32[16,1,49152]{2,1,0:T(1,128)} %copy.57), calls=%async_computation.3 | async-start | bytes 6291456 | tf_op jit(solution)/shard_map/all_to_all | solution.py:56
  239.2 1.9 copy-start.3
  243.1 2.1 copy-start.4
  243.5 1.7 copy-start
  258.4 18.0 %all-to-all-start.4 = ((bf16[16,16,2,2048]{3,1,0,2:T(8,128)(2,1)}), bf16[16,16,2,2048]{3,1,0,2:T(8,128)(2,1)}, u32[]{:S(2)}, u32[]{:S(2)}) async-start(bf16[16,16,2,2048]{3,1,0,2:T(8,128)(2,1)} %copy.58), calls=%async_computation.4 | async-start | bytes 4194304 | tf_op jit(solution)/shard_map/all_to_all | solution.py:94
  276.4 6.7 %all-to-all-start.8 = ((bf16[16,16,2,2048]{3,1,0,2:T(8,128)(2,1)}), bf16[16,16,2,2048]{3,1,0,2:T(8,128)(2,1)S(1)}, u32[]{:S(2)}, u32[]{:S(2)}) async-start(bf16[16,16,2,2048]{3,1,0,2:T(8,128)(2,1)} %copy.64), calls=%async_computation.8 | async-start | bytes 4194304 | tf_op jit(solution)/shard_map/all_to_all | solution.py:94
  283.1 40.3 %all-to-all-start.5 = ((bf16[16,16,2048]{2,1,0:T(8,128)(2,1)}), bf16[16,16,2048]{2,1,0:T(8,128)(2,1)S(1)}, u32[]{:S(2)}, u32[]{:S(2)}) async-start(bf16[16,16,2048]{2,1,0:T(8,128)(2,1)} %fusion.25), calls=%async_computation.5 | async-start | bytes 2097152 | tf_op jit(solution)/shard_map/all_to_all | solution.py:98
  298.5 31.8 %copy-start.8 = (f32[2,16,8]{1,2,0:T(8,128)S(1)}, f32[2,16,8]{1,2,0:T(8,128)}, u32[]{:S(2)}) copy-start(f32[2,16,8]{1,2,0:T(8,128)} %param.8) | copy-start | bytes 3076
  298.6 32.2 %copy-start.6 = (f32[3,2048]{1,0:T(4,128)S(1)}, f32[3,2048]{1,0:T(4,128)}, u32[]{:S(2)}) copy-start(f32[3,2048]{1,0:T(4,128)} %add_multiply_fusion) | copy-start | bytes 73732
  323.4 30.5 %all-to-all-start.9 = ((bf16[16,16,2048]{2,1,0:T(8,128)(2,1)}), bf16[16,16,2048]{2,1,0:T(8,128)(2,1)S(1)}, u32[]{:S(2)}, u32[]{:S(2)}) async-start(bf16[16,16,2048]{2,1,0:T(8,128)(2,1)} %fusion.26), calls=%async_computation.9 | async-start | bytes 2097152 | tf_op jit(solution)/shard_map/all_to_all | solution.py:98
where the time goes:
time: 357 us; the launch traced here: 355 us
  waiting for transfers between devices  167 us (47%)
  starting transfers between devices  65 us (18%)
  local copies, waits for them, and re-layouts  60.7 us (17%)
  other arithmetic  37.4 us (10%)
  matrix products  17.6 us (5%)
  blocking collectives  4.77 us (1%)
    all_to_all x1, waiting for transfers between devices, local(): lax.all_to_all(own_master.reshape(experts, -1), 'ep', split_axis=0, conca...  57.6 us
    all_to_all x1, waiting for transfers between devices, local(): lax.all_to_all(spread[arrive_from], 'ep', split_axis=0, concat_axis=0, ti...  50.5 us
    all_to_all x2, waiting for transfers between devices, local(): lax.all_to_all(summed, 'ep', split_axis=0, concat_axis=0, tiled=True)  45.4 us
    all_to_all x2, starting transfers between devices, local(): lax.all_to_all(summed, 'ep', split_axis=0, concat_axis=0, tiled=True)  22.3 us
    all_to_all x1, other arithmetic, local(): lax.all_to_all(spread[arrive_from], 'ep', split_axis=0, concat_axis=0, ti...  20.1 us
    all_to_all x1, starting transfers between devices, local(): lax.all_to_all(spread[arrive_from], 'ep', split_axis=0, concat_axis=0, ti...  14.2 us
    all_to_all x2, waiting for transfers between devices, local(): lax.all_to_all(outgoing, 'ep', split_axis=0, concat_axis=0, tiled=True)  13.7 us
    reshape x4, local copies, waits for them, and re-layouts, local(): running.astype(jnp.bfloat16).reshape(experts, capacity, 2, out_width)  13.6 us
  transfers between devices with their start and end apart: 9, of which 6 were waited for; matrix products, arithmetic and copies ran while one was open for 14% of the time, Pallas kernels for 0%

commit v1 on v0

--- a/solution.py
+++ b/solution.py
@@ -1,6 +1,10 @@
+import functools
+
 import jax
 import jax.numpy as jnp
 from jax import lax
+from jax.experimental import pallas as pl
+from jax.experimental.pallas import tpu as pltpu
 from jax.sharding import PartitionSpec as P
 
 Q_BLOCK = 128
@@ -108,6 +112,431 @@
     return (jnp.stack(results), level_output, new_grid[None])
 
 
+EXTRA_ROWS = 16
+
+
+def split3(value):
+    high = value.astype(jnp.bfloat16)
+    rest = value - high.astype(jnp.float32)
+    middle = rest.astype(jnp.bfloat16)
+    low = (rest - middle.astype(jnp.float32)).astype(jnp.bfloat16)
+    return high, middle, low
+
+
+def raw_levels(weights, step_grid):
+    blocks = weights.reshape(step_grid.shape[0], Q_BLOCK, weights.shape[-1])
+    nearest = jnp.floor(blocks / step_grid[:, None, :] + 0.5)
+    return jnp.clip(nearest, -127.0, 127.0).reshape(weights.shape)
+
+
+def requantize_kernel(master_ref, piece_ref):
+    weights = master_ref[...]
+    rows = weights.shape[0]
+    step_grid = grid_of(weights)
+    levels = raw_levels(weights, step_grid)
+    piece_ref[0, 0:rows, :] = (levels * 0.0078125).astype(jnp.bfloat16)
+    high, middle, low = split3(step_grid)
+    blocks = step_grid.shape[0]
+    fill = jnp.zeros((EXTRA_ROWS - 3 * blocks, weights.shape[1]), jnp.float32)
+    extra = jnp.concatenate(
+        [high.astype(jnp.float32), middle.astype(jnp.float32), low.astype(jnp.float32), fill], axis=0
+    )
+    piece_ref[0, rows : rows + EXTRA_ROWS, :] = extra.astype(jnp.bfloat16)
+
+
+def greet(targets):
+    barrier = pltpu.get_barrier_semaphore()
+    for target in targets:
+        pl.semaphore_signal(
+            barrier, inc=1, device_id=target, device_id_type=pl.DeviceIdType.MESH
+        )
+    pl.semaphore_wait(barrier, len(targets))
+
+
+def dispatch_kernel(
+    experts,
+    outgoing_ref,
+    pieces_ref,
+    arriving_ref,
+    spread_ref,
+    token_send,
+    token_recv,
+    piece_send,
+    piece_recv,
+    local_sem,
+):
+    me = lax.axis_index("ep")
+    core = lax.axis_index("sub")
+    half = arriving_ref.shape[-1]
+    everyone = []
+    for offset in range(experts):
+        for flip in range(2):
+            if offset or flip:
+                everyone.append(
+                    {"ep": lax.rem(me + offset, experts), "sub": lax.rem(core + flip, 2)}
+                )
+    greet(everyone)
+
+    def token_copy(offset, flip):
+        target = lax.rem(me + offset, experts)
+        side = lax.rem(core + flip, 2)
+        columns = pl.ds(pl.multiple_of(side * half, 128), half)
+        return pltpu.make_async_remote_copy(
+            src_ref=outgoing_ref.at[target, :, :, columns],
+            dst_ref=arriving_ref.at[:, core, me],
+            send_sem=token_send.at[offset, flip],
+            recv_sem=token_recv.at[offset, flip],
+            device_id={"ep": target, "sub": side},
+            device_id_type=pl.DeviceIdType.MESH,
+        )
+
+    def piece_copy(offset):
+        target = lax.rem(me + offset, experts)
+        return pltpu.make_async_remote_copy(
+            src_ref=pieces_ref.at[target],
+            dst_ref=spread_ref.at[me],
+            send_sem=piece_send.at[offset],
+            recv_sem=piece_recv.at[offset],
+            device_id={"ep": target, "sub": core},
+            device_id_type=pl.DeviceIdType.MESH,
+        )
+
+    own_tokens = pltpu.make_async_copy(
+        outgoing_ref.at[me, :, :, pl.ds(pl.multiple_of(core * half, 128), half)],
+        arriving_ref.at[:, core, me],
+        local_sem.at[0],
+    )
+    own_piece = pltpu.make_async_copy(pieces_ref.at[me], spread_ref.at[me], local_sem.at[1])
+    token_copies = [
+        token_copy(offset, flip) for offset in range(experts) for flip in range(2) if offset or flip
+    ]
+    piece_copies = [piece_copy(offset) for offset in range(1, experts)]
+    for copy in token_copies:
+        copy.start()
+    own_tokens.start()
+    for copy in piece_copies:
+        copy.start()
+    own_piece.start()
+    own_tokens.wait()
+    own_piece.wait()
+    for copy in token_copies + piece_copies:
+        copy.wait()
+
+
+def serve_kernel(active_ref, rows_ref, master_ref, stale_ref, out_ref):
+    weights = master_ref[...]
+    stale_grid = stale_ref[...]
+    new_grid = grid_of(weights)
+    stale_levels = raw_levels(weights, stale_grid)
+    new_levels = raw_levels(weights, new_grid)
+    for step in range(rows_ref.shape[0]):
+        moved = active_ref[step] > 0
+        step_grid = jnp.where(moved, new_grid, stale_grid)
+        levels = jnp.where(moved, new_levels, stale_levels).astype(jnp.bfloat16)
+        total = None
+        for block in range(step_grid.shape[0]):
+            here = slice(block * Q_BLOCK, (block + 1) * Q_BLOCK)
+            product = jnp.dot(
+                rows_ref[step, :, here], levels[here], preferred_element_type=jnp.float32
+            )
+            product = product * step_grid[block : block + 1, :]
+            total = product if total is None else total + product
+        out_ref[step] = total.astype(jnp.bfloat16)
+
+
+def combine_kernel(
+    experts,
+    partial_ref,
+    chosen_ref,
+    mixed_ref,
+    arrived_ref,
+    other_ref,
+    send_one,
+    recv_one,
+    send_two,
+    recv_two,
+    send_three,
+    recv_three,
+    other_sems,
+    one_sems,
+    two_sems,
+    three_sems,
+    piece_send,
+    piece_recv,
+    local_sem,
+):
+    me = lax.axis_index("ep")
+    core = lax.axis_index("sub")
+    planes = experts // 4
+    x = lax.rem(me, 2)
+    y = lax.rem(me // 2, 2)
+    z = me // 4
+    half = partial_ref.shape[-1] // 2
+    piece_columns = chosen_ref.shape[-1]
+    MESH = pl.DeviceIdType.MESH
+    peers = [{"ep": lax.rem(me + offset, experts), "sub": core} for offset in range(1, experts)]
+    partner = {"ep": me, "sub": 1 - core}
+    greet(peers + [partner])
+    sides = [slice(0, half), slice(half, 2 * half)]
+    across_x = {"ep": z * 4 + y * 2 + (1 - x), "sub": core}
+    across_y = {"ep": z * 4 + (1 - y) * 2 + x, "sub": core}
+
+    other_copies = []
+    for side in range(2):
+        copy = pltpu.make_async_remote_copy(
+            src_ref=partial_ref.at[:, 1 - core, :, :, sides[side]],
+            dst_ref=other_ref.at[:, :, :, sides[side]],
+            send_sem=other_sems.at[0, side],
+            recv_sem=other_sems.at[1, side],
+            device_id=partner,
+            device_id_type=MESH,
+        )
+        copy.start()
+        other_copies.append(copy)
+
+    columns = pl.ds(pl.multiple_of(me * piece_columns, 128), piece_columns)
+    piece_copies = []
+    for offset in range(1, experts):
+        target = lax.rem(me + offset, experts)
+        copy = pltpu.make_async_remote_copy(
+            src_ref=chosen_ref.at[target],
+            dst_ref=arrived_ref.at[:, columns],
+            send_sem=piece_send.at[offset],
+            recv_sem=piece_recv.at[offset],
+            device_id={"ep": target, "sub": core},
+            device_id_type=MESH,
+        )
+        piece_copies.append(copy)
+    own_piece = pltpu.make_async_copy(chosen_ref.at[me], arrived_ref.at[:, columns], local_sem.at[0])
+
+    def pair(target, side):
+        here = sides[side]
+        return partial_ref[:, core, target, :, here].astype(jnp.float32) + other_ref[
+            :, target, :, here
+        ].astype(jnp.float32)
+
+    def send(source, landing, sems, side, device):
+        copy = pltpu.make_async_remote_copy(
+            src_ref=source.at[side],
+            dst_ref=landing.at[side],
+            send_sem=sems.at[0, side],
+            recv_sem=sems.at[1, side],
+            device_id=device,
+            device_id_type=MESH,
+        )
+        copy.start()
+        return copy
+
+    one_copies = []
+    for side in range(2):
+        other_copies[side].wait()
+
+        def first(number, carry, side=side):
+            plane, place = number // 2, lax.rem(number, 2)
+            if side == 0:
+                target = plane * 4 + place * 2 + (1 - x)
+            else:
+                target = plane * 4 + (1 - y) * 2 + place
+            send_one[side, number] = pair(target, side).astype(jnp.bfloat16)
+            return carry
+
+        lax.fori_loop(0, 2 * planes, first, 0)
+        one_copies.append(
+            send(send_one, recv_one, one_sems, side, across_x if side == 0 else across_y)
+        )
+
+    for copy in piece_copies:
+        copy.start()
+    own_piece.start()
+
+    two_copies = []
+    for side in range(2):
+        one_copies[side].wait()
+
+        def second(plane, carry, side=side):
+            if side == 0:
+                target, number = plane * 4 + (1 - y) * 2 + x, plane * 2 + (1 - y)
+            else:
+                target, number = plane * 4 + y * 2 + (1 - x), plane * 2 + (1 - x)
+            value = pair(target, side) + recv_one[side, number].astype(jnp.float32)
+            send_two[side, plane] = value.astype(jnp.bfloat16)
+            return carry
+
+        lax.fori_loop(0, planes, second, 0)
+        two_copies.append(
+            send(send_two, recv_two, two_sems, side, across_y if side == 0 else across_x)
+        )
+
+    def third_value(plane, side):
+        target = plane * 4 + y * 2 + x
+        number = plane * 2 + (y if side == 0 else x)
+        return (
+            pair(target, side)
+            + recv_one[side, number].astype(jnp.float32)
+            + recv_two[side, plane].astype(jnp.float32)
+        )
+
+    for side in range(2):
+        two_copies[side].wait()
+    three_copies = []
+    for offset in range(1, planes):
+        plane = lax.rem(z + offset, planes)
+        for side in range(2):
+            send_three[offset - 1, :, :, sides[side]] = third_value(plane, side).astype(
+                jnp.bfloat16
+            )
+        copy = pltpu.make_async_remote_copy(
+            src_ref=send_three.at[offset - 1],
+            dst_ref=recv_three.at[offset - 1],
+            send_sem=three_sems.at[0, offset],
+            recv_sem=three_sems.at[1, offset],
+            device_id={"ep": plane * 4 + y * 2 + x, "sub": core},
+            device_id_type=MESH,
+        )
+        copy.start()
+        three_copies.append(copy)
+    for copy in three_copies:
+        copy.wait()
+    for side in range(2):
+        total = third_value(z, side)
+        for offset in range(1, planes):
+            total = total + recv_three[offset - 1, :, :, sides[side]].astype(jnp.float32)
+        mixed_ref[:, :, sides[side]] = total.astype(jnp.bfloat16)
+    own_piece.wait()
+    for copy in piece_copies:
+        copy.wait()
+
+
+def local_small(expert_inputs, routes, route_weights, master, old_steps, move_list):
+    experts = lax.axis_size("ep")
+    my_index = lax.axis_index("ep")
+    steps, tokens, top, inner = expert_inputs.shape
+    half, width = master.shape[1:]
+    piece_columns = width // experts
+    piece_rows = half + EXTRA_ROWS
+    any_space = pl.BlockSpec(memory_space=pl.ANY)
+    vmem = pl.BlockSpec(memory_space=pltpu.VMEM)
+    expert_column, old_column = move_list[:, 0], move_list[:, 1]
+    new_column, step_column = move_list[:, 2], move_list[:, 3]
+    all_experts = jnp.arange(experts, dtype=jnp.int32)
+    old_owner = lookup(expert_column, old_column, all_experts)
+    arrive_from = lookup(new_column, old_column, all_experts)
+    leave_step = lookup(old_column, step_column, jnp.reshape(my_index, (1,)))[0]
+    active = (jnp.arange(steps, dtype=jnp.int32) >= leave_step).astype(jnp.int32)
+
+    pieces = pl.pallas_call(
+        requantize_kernel,
+        out_shape=jax.ShapeDtypeStruct((experts, piece_rows, piece_columns), jnp.bfloat16),
+        grid=(experts,),
+        in_specs=[pl.BlockSpec((half, piece_columns), lambda i: (0, i))],
+        out_specs=pl.BlockSpec((1, piece_rows, piece_columns), lambda i: (i, 0, 0)),
+    )(master[0])
+
+    pairs = steps * tokens * top
+    ids = routes.reshape(pairs)
+    target = jnp.sum(
+        jnp.where(ids[:, None] == all_experts[None, :], old_owner[None, :], 0), axis=1
+    )
+    pair_numbers = jnp.arange(pairs, dtype=jnp.int32)
+    slot_numbers = jnp.arange(experts * steps * tokens, dtype=jnp.int32)
+    slot = target * (steps * tokens) + pair_numbers // top
+    selector = (slot[None, :] == slot_numbers[:, None]).astype(jnp.bfloat16)
+    rows = expert_inputs.reshape(pairs, inner).astype(jnp.float32)
+    rows = (rows * route_weights.reshape(pairs)[:, None]).astype(jnp.bfloat16)
+    outgoing = jnp.dot(selector, rows, preferred_element_type=jnp.float32).astype(jnp.bfloat16)
+    outgoing = outgoing.reshape(experts, steps, tokens, inner)
+
+    arriving, spread = pl.pallas_call(
+        functools.partial(dispatch_kernel, experts),
+        out_shape=(
+            jax.ShapeDtypeStruct((steps, 2, experts, tokens, half), jnp.bfloat16),
+            jax.ShapeDtypeStruct((experts, piece_rows, piece_columns), jnp.bfloat16),
+        ),
+        in_specs=[any_space, any_space],
+        out_specs=(any_space, any_space),
+        scratch_shapes=[
+            pltpu.SemaphoreType.DMA((experts, 2)),
+            pltpu.SemaphoreType.DMA((experts, 2)),
+            pltpu.SemaphoreType.DMA((experts,)),
+            pltpu.SemaphoreType.DMA((experts,)),
+            pltpu.SemaphoreType.DMA((2,)),
+        ],
+        compiler_params=pltpu.CompilerParams(collective_id=0, has_side_effects=True),
+    )(outgoing, pieces)
+
+    row_count = 2 * experts * tokens
+    tile = 256
+    blocks = half // Q_BLOCK
+    partial = pl.pallas_call(
+        serve_kernel,
+        out_shape=jax.ShapeDtypeStruct((steps, row_count, width), jnp.bfloat16),
+        grid=(width // tile,),
+        in_specs=[
+            pl.BlockSpec(memory_space=pltpu.SMEM),
+            pl.BlockSpec((steps, row_count, half), lambda i: (0, 0, 0)),
+            pl.BlockSpec((half, tile), lambda i: (0, i)),
+            pl.BlockSpec((blocks, tile), lambda i: (0, i)),
+        ],
+        out_specs=pl.BlockSpec((steps, row_count, tile), lambda i: (0, 0, i)),
+        compiler_params=pltpu.CompilerParams(vmem_limit_bytes=40 * 1024 * 1024),
+    )(active, arriving.reshape(steps, row_count, half), master[0], old_steps[0])
+    partial = partial.reshape(steps, 2, experts, tokens, width)
+    chosen = spread[arrive_from]
+
+    planes = experts // 4
+    mixed, arrived = pl.pallas_call(
+        functools.partial(combine_kernel, experts),
+        out_shape=(
+            jax.ShapeDtypeStruct((steps, tokens, width), jnp.bfloat16),
+            jax.ShapeDtypeStruct((piece_rows, width), jnp.bfloat16),
+        ),
+        in_specs=[vmem, any_space],
+        out_specs=(vmem, any_space),
+        scratch_shapes=[
+            pltpu.VMEM((steps, experts, tokens, width), jnp.bfloat16),
+            pltpu.VMEM((2, 2 * planes, steps, tokens, width // 2), jnp.bfloat16),
+            pltpu.VMEM((2, 2 * planes, steps, tokens, width // 2), jnp.bfloat16),
+            pltpu.VMEM((2, planes, steps, tokens, width // 2), jnp.bfloat16),
+            pltpu.VMEM((2, planes, steps, tokens, width // 2), jnp.bfloat16),
+            pltpu.VMEM((planes - 1, steps, tokens, width), jnp.bfloat16),
+            pltpu.VMEM((planes - 1, steps, tokens, width), jnp.bfloat16),
+            pltpu.SemaphoreType.DMA((2, 2)),
+            pltpu.SemaphoreType.DMA((2, 2)),
+            pltpu.SemaphoreType.DMA((2, 2)),
+            pltpu.SemaphoreType.DMA((2, planes)),
+            pltpu.SemaphoreType.DMA((experts,)),
+            pltpu.SemaphoreType.DMA((experts,)),
+            pltpu.SemaphoreType.DMA((1,)),
+        ],
+        compiler_params=pltpu.CompilerParams(
+            collective_id=1, has_side_effects=True, vmem_limit_bytes=48 * 1024 * 1024
+        ),
+    )(partial, chosen)
+    parts = arrived[half : half + 3 * blocks].astype(jnp.float32).reshape(3, blocks, width)
+    new_steps = (parts[0] + parts[1]) + parts[2]
+    return mixed, arrived[:half][None], new_steps[None]
+
+
+def body_for(mesh):
+    def body(expert_inputs, routes, route_weights, master, old_steps, move_list):
+        experts, cores = mesh.shape["ep"], mesh.shape["sub"]
+        tokens, top = routes.shape[1:]
+        half, width = master.shape[1:]
+        fits = (
+            experts % 4 == 0
+            and experts <= 16
+            and cores == 2
+            and tokens % 16 == 0
+            and width % (experts * 128) == 0
+            and half % Q_BLOCK == 0
+            and 3 * (half // Q_BLOCK) <= EXTRA_ROWS
+        )
+        chosen = local_small if fits else local
+        return chosen(expert_inputs, routes, route_weights, master, old_steps, move_list)
+
+    return body
+
+
 def solution(mesh):
     placed = (
         P(None, ("groups", "ep", "sub"), None, None),
@@ -118,7 +547,7 @@
         P(),
     )
     return jax.shard_map(
-        local,
+        body_for(mesh),
         mesh=mesh,
         in_specs=placed,
         out_specs=(

time: 357 us -> 156 us (0.44)
  waiting for transfers between devices: 167 us -> 0 us
  Pallas kernels: 0 us -> 139 us
  starting transfers between devices: 65 us -> 0 us
  local copies, waits for them, and re-layouts: 60.7 us -> 11.7 us
  other arithmetic: 37.4 us -> 2.37 us
  matrix products: 17.6 us -> 2.34 us
  blocking collectives: 4.77 us -> 0 us
    all_to_all x9 -> x0, waiting for transfers between devices: 167 us -> none  [the longest x1 57.6 us: local(): lax.all_to_all(own_master.reshape(experts, -1), 'ep', split_axis=0, conca...]
    pallas_call x0 -> x4, Pallas kernels: none -> 139 us  [the longest x1 73.1 us: local_small(): pl.pallas_call(functools.partial(combine_kernel, experts), out_shape=(jax...]
    all_to_all x9 -> x0, starting transfers between devices: 65 us -> none  [the longest x2 22.3 us: local(): lax.all_to_all(summed, 'ep', split_axis=0, concat_axis=0, tiled=True)]
    reshape x10 -> x0, local copies, waits for them, and re-layouts: 22.2 us -> none  [the longest x4 13.6 us: local(): running.astype(jnp.bfloat16).reshape(experts, capacity, 2, out_width)]
    all_to_all x1 -> x0, other arithmetic: 20.1 us -> none  [local(): lax.all_to_all(spread[arrive_from], 'ep', split_axis=0, concat_axis=0, ti...]
    all_to_all x6 -> x0, local copies, waits for them, and re-layouts: 17.4 us -> none  [the longest x1 6.84 us: local(): lax.all_to_all(spread[arrive_from], 'ep', split_axis=0, concat_axis=0, ti...]
    dot_general x6 -> x1, matrix products: 17.6 us -> 2.34 us  [local_small(): jnp.dot(selector, rows, preferred_element_type=jnp.float32)]
    convert_element_type x5 -> x2, other arithmetic: 6.48 us -> 0.66 us  [the longest x1 0.65 us: local_small(): (jnp.arange(steps, dtype=jnp.int32) >= leave_step).astype(jnp.int32)]
  transfers between devices with their start and end apart: 9 -> 0, of which waited for: 6 -> 0; matrix products, arithmetic and copies ran while one was open for 14% -> 0% of each run, Pallas kernels for 0% -> 0%
where the time goes in v1:
time: 156 us
  Pallas kernels  139 us (89%)
  local copies, waits for them, and re-layouts  11.7 us (8%)
  other arithmetic  2.37 us (2%)
  matrix products  2.34 us (2%)
    pallas_call x1, Pallas kernels, local_small(): pl.pallas_call(functools.partial(combine_kernel, experts), out_shape=(jax...  73.1 us
    pallas_call x1, Pallas kernels, local_small(): pl.pallas_call(functools.partial(dispatch_kernel, experts), out_shape=(ja...  48.8 us
    pallas_call x1, Pallas kernels, local_small(): pl.pallas_call(requantize_kernel, out_shape=jax.ShapeDtypeStruct((experts...  9.86 us
    pallas_call x1, Pallas kernels, local_small(): pl.pallas_call(serve_kernel, out_shape=jax.ShapeDtypeStruct((steps, row_c...  6.86 us
    unnamed x13, local copies, waits for them, and re-layouts  6.65 us
    gather x1, local copies, waits for them, and re-layouts, local_small(): chosen = spread[arrive_from]  3.55 us

profile of v1, /device:TPU:0, one launch (start us, length us, event | category | flops | bytes accessed | tf_op | source)
XLA Modules:
  0.0 155.8 jit_solution(8867803490146811630)
XLA Ops:
  0.6 1.5 slice_bitcast_fusion.2
  2.1 0.1 select_reduce_fusion.1
  2.2 0.7 compare_convert_fusion.active_ref
  2.9 0.8 copy.13
  3.7 0.1 eq.77
  3.8 0.1 select_reduce_fusion
  3.9 0.8 copy.14
  4.6 0.1 mul.22
  4.7 0.8 copy.18
  5.5 2.3 %convolution_convert_fusion = bf16[512,768]{1,0:T(8,128)(2,1)} fusion(bf16[256,768]{1,0:T(8,128)(2,1)} %bitcast.29, f32[256]{0:T(256)S(1)} %mul.22, s32[256]{0:T(256)S(1)} %fusion.5), kind=kOutput, calls=%fused_computation.2 | convolution fusion | flops 202440704 | bytes 1181696 | tf_op jit(solution)/shard_map/dot_general | solution.py:446
  7.8 9.9 %shard_map.85.pieces_ref = bf16[16,400,128]{2,1,0:T(8,128)(2,1)} custom-call(f32[384,2048]{1,0:T(8,128)} %bitcast.24), custom_call_target="tpu_custom_call" | custom-call | tf_op jit(solution)/shard_map/pallas_call | solution.py:427
  17.7 48.8 %shard_map.86 = (bf16[2,2,16,16,384]{4,3,2,1,0:T(8,128)(2,1)}, bf16[16,400,128]{2,1,0:T(8,128)(2,1)}) custom-call(bf16[16,2,16,768]{3,2,1,0:T(8,128)(2,1)} %bitcast.28, bf16[16,400,128]{2,1,0:T(8,128)(2,1)} %shard_map.85.pieces_ref), custom_call_target="tpu_custom_call" | custom-call | tf_op jit(solution)/shard_map/pallas_call | solution.py:449
  66.5 0.0 copy-start.1
  66.5 3.5 %gather_fusion = bf16[16,400,128]{2,1,0:T(8,128)(2,1)} fusion(bf16[16,400,128]{2,1,0:T(8,128)(2,1)} %get-tuple-element.8, s32[1024]{0:T(1024)S(1)} %pad_clamp_fusion), kind=kCustom, calls=%fused_computation | custom fusion | bytes 3276864 | tf_op jit(solution)/shard_map/gather | solution.py:484
  70.1 0.0 copy-done.1
  70.1 0.0 copy-start.3
  70.1 1.1 copy-done.3
  71.2 0.0 copy-start.2
  71.2 6.9 %shard_map.87 = bf16[2,512,2048]{2,1,0:T(8,128)(2,1)S(1)} custom-call(s32[2]{0:T(128)S(1)} %compare_convert_fusion.active_ref, bf16[2,512,384]{2,1,0:T(8,128)(2,1)S(1)} %bitcast.26, f32[384,2048]{1,0:T(8,128)S(1)} %bitcast.25, f32[3,2048]{1,0:T(4,128)S(1)} %bitcast.27), custom_call_target="tpu_custom_call" | custom-call | tf_op jit(solution)/shard_map/pallas_call | solution.py:470
  78.1 0.0 copy-start
  78.1 1.9 %copy-done = bf16[2,512,2048]{2,1,0:T(8,128)(2,1)} copy-done((bf16[2,512,2048]{2,1,0:T(8,128)(2,1)}, bf16[2,512,2048]{2,1,0:T(8,128)(2,1)S(1)}, u32[]{:S(2)}) %copy-start) | copy-done | bytes 4194328
  80.0 0.0 copy-done.2
  80.0 73.1 %shard_map.88 = (bf16[2,16,2048]{2,1,0:T(8,128)(2,1)S(1)}, bf16[400,2048]{1,0:T(8,128)(2,1)S(1)}) custom-call(bf16[2,2,16,16,2048]{4,3,2,1,0:T(8,128)(2,1)} %bitcast.23, bf16[16,400,128]{2,1,0:T(8,128)(2,1)S(1)} %copy-done.2), custom_call_target="tpu_custom_call" | custom-call | tf_op jit(solution)/shard_map/pallas_call | solution.py:487
  153.2 1.3 slice_bitcast_fusion
  154.5 0.6 copy.15
  155.1 0.7 copy.20
  (5 shorter events, 0.0 us)
Async XLA Ops:
  66.5 3.6 %copy-start.1 = (f32[1,384,2048]{2,1,0:T(8,128)S(1)}, f32[1,384,2048]{2,1,0:T(8,128)}, u32[]{:S(2)}) copy-start(f32[1,384,2048]{2,1,0:T(8,128)} %param.9) | copy-start | bytes 9437188
  70.1 1.1 copy-start.3
  71.2 8.8 %copy-start.2 = (bf16[16,400,128]{2,1,0:T(8,128)(2,1)S(1)}, bf16[16,400,128]{2,1,0:T(8,128)(2,1)}, u32[]{:S(2)}) copy-start(bf16[16,400,128]{2,1,0:T(8,128)(2,1)} %gather_fusion) | copy-start | bytes 4915204
  78.1 1.9 %copy-start = (bf16[2,512,2048]{2,1,0:T(8,128)(2,1)}, bf16[2,512,2048]{2,1,0:T(8,128)(2,1)S(1)}, u32[]{:S(2)}) copy-start(bf16[2,512,2048]{2,1,0:T(8,128)(2,1)S(1)} %shard_map.87) | copy-start | bytes 12582916

commit v2 on v1

--- a/solution.py
+++ b/solution.py
@@ -129,21 +129,6 @@
     return jnp.clip(nearest, -127.0, 127.0).reshape(weights.shape)
 
 
-def requantize_kernel(master_ref, piece_ref):
-    weights = master_ref[...]
-    rows = weights.shape[0]
-    step_grid = grid_of(weights)
-    levels = raw_levels(weights, step_grid)
-    piece_ref[0, 0:rows, :] = (levels * 0.0078125).astype(jnp.bfloat16)
-    high, middle, low = split3(step_grid)
-    blocks = step_grid.shape[0]
-    fill = jnp.zeros((EXTRA_ROWS - 3 * blocks, weights.shape[1]), jnp.float32)
-    extra = jnp.concatenate(
-        [high.astype(jnp.float32), middle.astype(jnp.float32), low.astype(jnp.float32), fill], axis=0
-    )
-    piece_ref[0, rows : rows + EXTRA_ROWS, :] = extra.astype(jnp.bfloat16)
-
-
 def greet(targets):
     barrier = pltpu.get_barrier_semaphore()
     for target in targets:
@@ -153,21 +138,51 @@
     pl.semaphore_wait(barrier, len(targets))
 
 
-def dispatch_kernel(
+def whole_kernel(
     experts,
+    arrive_ref,
+    active_ref,
     outgoing_ref,
+    master_ref,
+    stale_ref,
+    mixed_ref,
+    arrived_ref,
+    arriving_ref,
+    levels_ref,
+    grids_ref,
     pieces_ref,
-    arriving_ref,
     spread_ref,
+    chosen_ref,
+    partial_ref,
+    other_ref,
+    send_one,
+    recv_one,
+    send_two,
+    recv_two,
+    send_three,
+    recv_three,
     token_send,
     token_recv,
-    piece_send,
-    piece_recv,
+    spread_sems,
+    move_sems,
+    other_sems,
+    one_sems,
+    two_sems,
+    three_sems,
     local_sem,
 ):
     me = lax.axis_index("ep")
     core = lax.axis_index("sub")
-    half = arriving_ref.shape[-1]
+    steps, _, _, tokens, rows = arriving_ref.shape
+    blocks = rows // Q_BLOCK
+    width = partial_ref.shape[-1]
+    piece_columns = width // experts
+    planes = experts // 4
+    x = lax.rem(me, 2)
+    y = lax.rem(me // 2, 2)
+    z = me // 4
+    half = width // 2
+    MESH = pl.DeviceIdType.MESH
     everyone = []
     for offset in range(experts):
         for flip in range(2):
@@ -180,134 +195,109 @@
     def token_copy(offset, flip):
         target = lax.rem(me + offset, experts)
         side = lax.rem(core + flip, 2)
-        columns = pl.ds(pl.multiple_of(side * half, 128), half)
+        columns = pl.ds(pl.multiple_of(side * rows, 128), rows)
         return pltpu.make_async_remote_copy(
             src_ref=outgoing_ref.at[target, :, :, columns],
             dst_ref=arriving_ref.at[:, core, me],
             send_sem=token_send.at[offset, flip],
             recv_sem=token_recv.at[offset, flip],
             device_id={"ep": target, "sub": side},
-            device_id_type=pl.DeviceIdType.MESH,
-        )
-
-    def piece_copy(offset):
-        target = lax.rem(me + offset, experts)
-        return pltpu.make_async_remote_copy(
-            src_ref=pieces_ref.at[target],
-            dst_ref=spread_ref.at[me],
-            send_sem=piece_send.at[offset],
-            recv_sem=piece_recv.at[offset],
-            device_id={"ep": target, "sub": core},
-            device_id_type=pl.DeviceIdType.MESH,
-        )
-
+            device_id_type=MESH,
+        )
+
+    token_copies = [
+        token_copy(offset, flip) for offset in range(experts) for flip in range(2) if offset or flip
+    ]
+    for copy in token_copies:
+        copy.start()
     own_tokens = pltpu.make_async_copy(
-        outgoing_ref.at[me, :, :, pl.ds(pl.multiple_of(core * half, 128), half)],
+        outgoing_ref.at[me, :, :, pl.ds(pl.multiple_of(core * rows, 128), rows)],
         arriving_ref.at[:, core, me],
         local_sem.at[0],
     )
-    own_piece = pltpu.make_async_copy(pieces_ref.at[me], spread_ref.at[me], local_sem.at[1])
-    token_copies = [
-        token_copy(offset, flip) for offset in range(experts) for flip in range(2) if offset or flip
-    ]
-    piece_copies = [piece_copy(offset) for offset in range(1, experts)]
+    own_tokens.start()
+
+    def requantize(piece, carry):
+        columns = pl.ds(pl.multiple_of(piece * piece_columns, 128), piece_columns)
+        weights = master_ref[:, columns]
+        stale_grid = stale_ref[:, columns]
+        new_grid = grid_of(weights)
+        new_levels = raw_levels(weights, new_grid)
+        stale_levels = raw_levels(weights, stale_grid)
+        pieces_ref[piece, 0:rows, :] = (new_levels * 0.0078125).astype(jnp.bfloat16)
+        high, middle, low = split3(new_grid)
+        fill = jnp.zeros((EXTRA_ROWS - 3 * blocks, piece_columns), jnp.float32)
+        parts = [part.astype(jnp.float32) for part in (high, middle, low)]
+        extra = jnp.concatenate(parts + [fill], axis=0)
+        pieces_ref[piece, rows : rows + EXTRA_ROWS, :] = extra.astype(jnp.bfloat16)
+        for step in range(steps):
+            moved = active_ref[step : step + 1, :] > 0
+            grids_ref[step, 0:blocks, columns] = jnp.where(moved, new_grid, stale_grid)
+            levels_ref[step, :, columns] = jnp.where(moved, new_levels, stale_levels).astype(
+                jnp.bfloat16
+            )
+        return carry
+
+    lax.fori_loop(0, experts, requantize, 0)
+
+    spread_copies = []
+    for offset in range(1, experts):
+        target = lax.rem(me + offset, experts)
+        copy = pltpu.make_async_remote_copy(
+            src_ref=pieces_ref.at[target],
+            dst_ref=spread_ref.at[me],
+            send_sem=spread_sems.at[0, offset],
+            recv_sem=spread_sems.at[1, offset],
+            device_id={"ep": target, "sub": core},
+            device_id_type=MESH,
+        )
+        copy.start()
+        spread_copies.append(copy)
+    own_spread = pltpu.make_async_copy(pieces_ref.at[me], spread_ref.at[me], local_sem.at[1])
+    own_spread.start()
+
+    own_tokens.wait()
     for copy in token_copies:
-        copy.start()
-    own_tokens.start()
-    for copy in piece_copies:
-        copy.start()
-    own_piece.start()
-    own_tokens.wait()
-    own_piece.wait()
-    for copy in token_copies + piece_copies:
-        copy.wait()
-
-
-def serve_kernel(active_ref, rows_ref, master_ref, stale_ref, out_ref):
-    weights = master_ref[...]
-    stale_grid = stale_ref[...]
-    new_grid = grid_of(weights)
-    stale_levels = raw_levels(weights, stale_grid)
-    new_levels = raw_levels(weights, new_grid)
-    for step in range(rows_ref.shape[0]):
-        moved = active_ref[step] > 0
-        step_grid = jnp.where(moved, new_grid, stale_grid)
-        levels = jnp.where(moved, new_levels, stale_levels).astype(jnp.bfloat16)
-        total = None
-        for block in range(step_grid.shape[0]):
-            here = slice(block * Q_BLOCK, (block + 1) * Q_BLOCK)
-            product = jnp.dot(
-                rows_ref[step, :, here], levels[here], preferred_element_type=jnp.float32
-            )
-            product = product * step_grid[block : block + 1, :]
-            total = product if total is None else total + product
-        out_ref[step] = total.astype(jnp.bfloat16)
-
-
-def combine_kernel(
-    experts,
-    partial_ref,
-    chosen_ref,
-    mixed_ref,
-    arrived_ref,
-    other_ref,
-    send_one,
-    recv_one,
-    send_two,
-    recv_two,
-    send_three,
-    recv_three,
-    other_sems,
-    one_sems,
-    two_sems,
-    three_sems,
-    piece_send,
-    piece_recv,
-    local_sem,
-):
-    me = lax.axis_index("ep")
-    core = lax.axis_index("sub")
-    planes = experts // 4
-    x = lax.rem(me, 2)
-    y = lax.rem(me // 2, 2)
-    z = me // 4
-    half = partial_ref.shape[-1] // 2
-    piece_columns = chosen_ref.shape[-1]
-    MESH = pl.DeviceIdType.MESH
-    peers = [{"ep": lax.rem(me + offset, experts), "sub": core} for offset in range(1, experts)]
-    partner = {"ep": me, "sub": 1 - core}
-    greet(peers + [partner])
+        copy.wait_recv()
+
+    tile = min(256, width)
+
+    def serve(number, carry):
+        columns = pl.ds(pl.multiple_of(number * tile, 128), tile)
+        for step in range(steps):
+            token_rows = arriving_ref[step].reshape(2 * experts * tokens, rows)
+            total = None
+            for block in range(blocks):
+                here = slice(block * Q_BLOCK, (block + 1) * Q_BLOCK)
+                product = jnp.dot(
+                    token_rows[:, here],
+                    levels_ref[step, here, columns],
+                    preferred_element_type=jnp.float32,
+                )
+                product = product * grids_ref[step, block : block + 1, columns]
+                total = product if total is None else total + product
+            partial_ref[step, :, :, :, columns] = total.reshape(
+                2, experts, tokens, tile
+            ).astype(jnp.bfloat16)
+        return carry
+
     sides = [slice(0, half), slice(half, 2 * half)]
     across_x = {"ep": z * 4 + y * 2 + (1 - x), "sub": core}
     across_y = {"ep": z * 4 + (1 - y) * 2 + x, "sub": core}
-
     other_copies = []
+    tiles = half // tile
     for side in range(2):
+        lax.fori_loop(side * tiles, (side + 1) * tiles, serve, 0)
         copy = pltpu.make_async_remote_copy(
             src_ref=partial_ref.at[:, 1 - core, :, :, sides[side]],
             dst_ref=other_ref.at[:, :, :, sides[side]],
             send_sem=other_sems.at[0, side],
             recv_sem=other_sems.at[1, side],
-            device_id=partner,
+            device_id={"ep": me, "sub": 1 - core},
             device_id_type=MESH,
         )
         copy.start()
         other_copies.append(copy)
-
-    columns = pl.ds(pl.multiple_of(me * piece_columns, 128), piece_columns)
-    piece_copies = []
-    for offset in range(1, experts):
-        target = lax.rem(me + offset, experts)
-        copy = pltpu.make_async_remote_copy(
-            src_ref=chosen_ref.at[target],
-            dst_ref=arrived_ref.at[:, columns],
-            send_sem=piece_send.at[offset],
-            recv_sem=piece_recv.at[offset],
-            device_id={"ep": target, "sub": core},
-            device_id_type=MESH,
-        )
-        piece_copies.append(copy)
-    own_piece = pltpu.make_async_copy(chosen_ref.at[me], arrived_ref.at[:, columns], local_sem.at[0])
 
     def pair(target, side):
         here = sides[side]
@@ -345,10 +335,6 @@
             send(send_one, recv_one, one_sems, side, across_x if side == 0 else across_y)
         )
 
-    for copy in piece_copies:
-        copy.start()
-    own_piece.start()
-
     two_copies = []
     for side in range(2):
         one_copies[side].wait()
@@ -375,6 +361,32 @@
             + recv_one[side, number].astype(jnp.float32)
             + recv_two[side, plane].astype(jnp.float32)
         )
+
+    own_spread.wait()
+    for copy in spread_copies:
+        copy.wait()
+
+    def choose(number, carry):
+        chosen_ref[number] = spread_ref[arrive_ref[number]]
+        return carry
+
+    lax.fori_loop(0, experts, choose, 0)
+    columns = pl.ds(pl.multiple_of(me * piece_columns, 128), piece_columns)
+    piece_copies = []
+    for offset in range(1, experts):
+        target = lax.rem(me + offset, experts)
+        copy = pltpu.make_async_remote_copy(
+            src_ref=chosen_ref.at[target],
+            dst_ref=arrived_ref.at[:, columns],
+            send_sem=move_sems.at[0, offset],
+            recv_sem=move_sems.at[1, offset],
+            device_id={"ep": target, "sub": core},
+            device_id_type=MESH,
+        )
+        copy.start()
+        piece_copies.append(copy)
+    own_piece = pltpu.make_async_copy(chosen_ref.at[me], arrived_ref.at[:, columns], local_sem.at[2])
+    own_piece.start()
 
     for side in range(2):
         two_copies[side].wait()
@@ -405,6 +417,8 @@
     own_piece.wait()
     for copy in piece_copies:
         copy.wait()
+    for copy in token_copies:
+        copy.wait_send()
 
 
 def local_small(expert_inputs, routes, route_weights, master, old_steps, move_list):
@@ -423,14 +437,7 @@
     arrive_from = lookup(new_column, old_column, all_experts)
     leave_step = lookup(old_column, step_column, jnp.reshape(my_index, (1,)))[0]
     active = (jnp.arange(steps, dtype=jnp.int32) >= leave_step).astype(jnp.int32)
-
-    pieces = pl.pallas_call(
-        requantize_kernel,
-        out_shape=jax.ShapeDtypeStruct((experts, piece_rows, piece_columns), jnp.bfloat16),
-        grid=(experts,),
-        in_specs=[pl.BlockSpec((half, piece_columns), lambda i: (0, i))],
-        out_specs=pl.BlockSpec((1, piece_rows, piece_columns), lambda i: (i, 0, 0)),
-    )(master[0])
+    active = jnp.broadcast_to(active[:, None], (steps, piece_columns))
 
     pairs = steps * tokens * top
     ids = routes.reshape(pairs)
@@ -446,72 +453,46 @@
     outgoing = jnp.dot(selector, rows, preferred_element_type=jnp.float32).astype(jnp.bfloat16)
     outgoing = outgoing.reshape(experts, steps, tokens, inner)
 
-    arriving, spread = pl.pallas_call(
-        functools.partial(dispatch_kernel, experts),
+    blocks = half // Q_BLOCK
+    planes = experts // 4
+    bf16 = jnp.bfloat16
+    mixed, arrived = pl.pallas_call(
+        functools.partial(whole_kernel, experts),
         out_shape=(
-            jax.ShapeDtypeStruct((steps, 2, experts, tokens, half), jnp.bfloat16),
-            jax.ShapeDtypeStruct((experts, piece_rows, piece_columns), jnp.bfloat16),
+            jax.ShapeDtypeStruct((steps, tokens, width), bf16),
+            jax.ShapeDtypeStruct((piece_rows, width), bf16),
         ),
-        in_specs=[any_space, any_space],
-        out_specs=(any_space, any_space),
+        in_specs=[pl.BlockSpec(memory_space=pltpu.SMEM), vmem, any_space, vmem, vmem],
+        out_specs=(vmem, any_space),
         scratch_shapes=[
+            pltpu.VMEM((steps, 2, experts, tokens, half), bf16),
+            pltpu.VMEM((steps, half, width), bf16),
+            pltpu.VMEM((steps, max(8, blocks), width), jnp.float32),
+            pltpu.VMEM((experts, piece_rows, piece_columns), bf16),
+            pltpu.VMEM((experts, piece_rows, piece_columns), bf16),
+            pltpu.VMEM((experts, piece_rows, piece_columns), bf16),
+            pltpu.VMEM((steps, 2, experts, tokens, width), bf16),
+            pltpu.VMEM((steps, experts, tokens, width), bf16),
+            pltpu.VMEM((2, 2 * planes, steps, tokens, width // 2), bf16),
+            pltpu.VMEM((2, 2 * planes, steps, tokens, width // 2), bf16),
+            pltpu.VMEM((2, planes, steps, tokens, width // 2), bf16),
+            pltpu.VMEM((2, planes, steps, tokens, width // 2), bf16),
+            pltpu.VMEM((planes - 1, steps, tokens, width), bf16),
+            pltpu.VMEM((planes - 1, steps, tokens, width), bf16),
             pltpu.SemaphoreType.DMA((experts, 2)),
             pltpu.SemaphoreType.DMA((experts, 2)),
-            pltpu.SemaphoreType.DMA((experts,)),
-            pltpu.SemaphoreType.DMA((experts,)),
-            pltpu.SemaphoreType.DMA((2,)),
-        ],
-        compiler_params=pltpu.CompilerParams(collective_id=0, has_side_effects=True),
-    )(outgoing, pieces)
-
-    row_count = 2 * experts * tokens
-    tile = 256
-    blocks = half // Q_BLOCK
-    partial = pl.pallas_call(
-        serve_kernel,
-        out_shape=jax.ShapeDtypeStruct((steps, row_count, width), jnp.bfloat16),
-        grid=(width // tile,),
-        in_specs=[
-            pl.BlockSpec(memory_space=pltpu.SMEM),
-            pl.BlockSpec((steps, row_count, half), lambda i: (0, 0, 0)),
-            pl.BlockSpec((half, tile), lambda i: (0, i)),
-            pl.BlockSpec((blocks, tile), lambda i: (0, i)),
-        ],
-        out_specs=pl.BlockSpec((steps, row_count, tile), lambda i: (0, 0, i)),
-        compiler_params=pltpu.CompilerParams(vmem_limit_bytes=40 * 1024 * 1024),
-    )(active, arriving.reshape(steps, row_count, half), master[0], old_steps[0])
-    partial = partial.reshape(steps, 2, experts, tokens, width)
-    chosen = spread[arrive_from]
-
-    planes = experts // 4
-    mixed, arrived = pl.pallas_call(
-        functools.partial(combine_kernel, experts),
-        out_shape=(
-            jax.ShapeDtypeStruct((steps, tokens, width), jnp.bfloat16),
-            jax.ShapeDtypeStruct((piece_rows, width), jnp.bfloat16),
-        ),
-        in_specs=[vmem, any_space],
-        out_specs=(vmem, any_space),
-        scratch_shapes=[
-            pltpu.VMEM((steps, experts, tokens, width), jnp.bfloat16),
-            pltpu.VMEM((2, 2 * planes, steps, tokens, width // 2), jnp.bfloat16),
-            pltpu.VMEM((2, 2 * planes, steps, tokens, width // 2), jnp.bfloat16),
-            pltpu.VMEM((2, planes, steps, tokens, width // 2), jnp.bfloat16),
-            pltpu.VMEM((2, planes, steps, tokens, width // 2), jnp.bfloat16),
-            pltpu.VMEM((planes - 1, steps, tokens, width), jnp.bfloat16),
-            pltpu.VMEM((planes - 1, steps, tokens, width), jnp.bfloat16),
+            pltpu.SemaphoreType.DMA((2, experts)),
+            pltpu.SemaphoreType.DMA((2, experts)),
             pltpu.SemaphoreType.DMA((2, 2)),
             pltpu.SemaphoreType.DMA((2, 2)),
             pltpu.SemaphoreType.DMA((2, 2)),
             pltpu.SemaphoreType.DMA((2, planes)),
-            pltpu.SemaphoreType.DMA((experts,)),
-            pltpu.SemaphoreType.DMA((experts,)),
-            pltpu.SemaphoreType.DMA((1,)),
+            pltpu.SemaphoreType.DMA((3,)),
         ],
         compiler_params=pltpu.CompilerParams(
-            collective_id=1, has_side_effects=True, vmem_limit_bytes=48 * 1024 * 1024
+            collective_id=0, has_side_effects=True, vmem_limit_bytes=52 * 1024 * 1024
         ),
-    )(partial, chosen)
+    )(arrive_from, active, outgoing, master[0], old_steps[0])
     parts = arrived[half : half + 3 * blocks].astype(jnp.float32).reshape(3, blocks, width)
     new_steps = (parts[0] + parts[1]) + parts[2]
     return mixed, arrived[:half][None], new_steps[None]

time: 156 us -> 131 us (0.84)
  the two profiles are of different devices: /device:TPU:0 before, /device:TPU:27 now
where the time goes in v2:
time: 131 us
  Pallas kernels  119 us (91%)
  local copies, waits for them, and re-layouts  6.56 us (5%)
  other arithmetic  3.2 us (2%)
  matrix products  1.46 us (1%)
    pallas_call x1, Pallas kernels, local_small(): pl.pallas_call(functools.partial(whole_kernel, experts), out_shape=(jax.S...  119 us
    unnamed x5, local copies, waits for them, and re-layouts  3.59 us
    broadcast_in_dim x1, local copies, waits for them, and re-layouts, local_small(): return (mixed, arrived[:half][None], new_steps[None])  2.73 us

profile of v2, /device:TPU:27, one launch (start us, length us, event | category | flops | bytes accessed | tf_op | source)
XLA Modules:
  0.0 130.7 jit_solution(16067365500366489348)
XLA Ops:
  0.6 1.5 %fusion.6 = (s32[]{:T(128)}, s32[16]{0:T(128)S(1)}, s32[16]{0:T(128)S(1)}, s32[16]{0:T(128)S(1)}) fusion(s32[16,4]{0,1:T(4,128)} %param.11, s32[]{:T(128)S(6)} %axis_index.15), kind=kLoop, calls=%fused_computation.25 | loop fusion | flops 47 | bytes 456 | tf_op jit(solution)/shard_map/reduce_sum | solution.py:34
  2.1 0.1 select_reduce_fusion.1
  2.2 0.7 compare_convert_fusion
  2.9 0.1 broadcast_in_dim.54.active_ref
  2.9 0.8 copy.13
  3.7 0.1 eq.81
  3.8 0.1 select_reduce_fusion
  3.9 0.8 copy.14
  4.7 0.1 mul.22
  4.8 0.8 copy.18
  5.5 1.5 %convolution_convert_fusion = bf16[512,768]{1,0:T(8,128)(2,1)S(1)} fusion(bf16[256,768]{1,0:T(8,128)(2,1)} %bitcast.20, f32[256]{0:T(256)S(1)} %mul.22, s32[256]{0:T(256)S(1)} %fusion.5), kind=kOutput, calls=%fused_computation.1 | convolution fusion | flops 202440704 | bytes 1181696 | tf_op jit(solution)/shard_map/dot_general | solution.py:453
  7.0 118.8 %shard_map.85 = (bf16[2,16,2048]{2,1,0:T(8,128)(2,1)S(1)}, bf16[400,2048]{1,0:T(8,128)(2,1)}) custom-call(s32[16]{0:T(128)S(1)} %get-tuple-element.17.arrive_ref, s32[2,128]{1,0:T(2,128)S(1)} %broadcast_in_dim.54.active_ref, bf16[16,2,16,768]{3,2,1,0:T(8,128)(2,1)S(1)} %bitcast.17, f32[384,2048]{1,0:T(8,128)} %bitcast.19, f32[3,2048]{1,0:T(4,128)S(1)} %bitcast.18), custom_call_target="tpu_custom_call" | custom-call | tf_op jit(solution)/shard_map/pallas_call | solution.py:459
  125.8 0.9 slice_convert_fusion
  126.7 2.7 %slice_bitcast_fusion = bf16[1,384,2048]{2,1,0:T(8,128)(2,1)} fusion(bf16[400,2048]{1,0:T(8,128)(2,1)} %get-tuple-element.6), kind=kLoop, calls=%fused_computation | loop fusion | bytes 3145728 | tf_op jit(solution)/shard_map/broadcast_in_dim | solution.py:498
  129.4 0.6 copy.15
  130.1 0.7 copy.20
  (2 shorter events, 0.0 us)

commit v3 on v2

--- a/solution.py
+++ b/solution.py
@@ -151,8 +151,9 @@
     levels_ref,
     grids_ref,
     pieces_ref,
-    spread_ref,
-    chosen_ref,
+    spread_refs,
+    chosen_refs,
+    weights_ref,
     partial_ref,
     other_ref,
     send_one,
@@ -183,6 +184,7 @@
     z = me // 4
     half = width // 2
     MESH = pl.DeviceIdType.MESH
+    order = sorted(range(1, experts), key=lambda offset: abs(offset - experts // 2))
     everyone = []
     for offset in range(experts):
         for flip in range(2):
@@ -190,6 +192,8 @@
                 everyone.append(
                     {"ep": lax.rem(me + offset, experts), "sub": lax.rem(core + flip, 2)}
                 )
+    own_master = pltpu.make_async_copy(master_ref, weights_ref, local_sem.at[0])
+    own_master.start()
     greet(everyone)
 
     def token_copy(offset, flip):
@@ -206,20 +210,21 @@
         )
 
     token_copies = [
-        token_copy(offset, flip) for offset in range(experts) for flip in range(2) if offset or flip
+        token_copy(offset, flip) for offset in order + [0] for flip in range(2) if offset or flip
     ]
     for copy in token_copies:
         copy.start()
     own_tokens = pltpu.make_async_copy(
         outgoing_ref.at[me, :, :, pl.ds(pl.multiple_of(core * rows, 128), rows)],
         arriving_ref.at[:, core, me],
-        local_sem.at[0],
+        local_sem.at[1],
     )
     own_tokens.start()
+    own_master.wait()
 
     def requantize(piece, carry):
         columns = pl.ds(pl.multiple_of(piece * piece_columns, 128), piece_columns)
-        weights = master_ref[:, columns]
+        weights = weights_ref[:, columns]
         stale_grid = stale_ref[:, columns]
         new_grid = grid_of(weights)
         new_levels = raw_levels(weights, new_grid)
@@ -240,21 +245,28 @@
 
     lax.fori_loop(0, experts, requantize, 0)
 
+    cut = rows // 2
+    shares = [slice(0, cut), slice(cut, rows + EXTRA_ROWS)]
     spread_copies = []
-    for offset in range(1, experts):
-        target = lax.rem(me + offset, experts)
-        copy = pltpu.make_async_remote_copy(
-            src_ref=pieces_ref.at[target],
-            dst_ref=spread_ref.at[me],
-            send_sem=spread_sems.at[0, offset],
-            recv_sem=spread_sems.at[1, offset],
-            device_id={"ep": target, "sub": core},
-            device_id_type=MESH,
-        )
-        copy.start()
-        spread_copies.append(copy)
-    own_spread = pltpu.make_async_copy(pieces_ref.at[me], spread_ref.at[me], local_sem.at[1])
-    own_spread.start()
+    for share in range(2):
+        copies = []
+        for offset in order:
+            target = lax.rem(me + offset, experts)
+            copy = pltpu.make_async_remote_copy(
+                src_ref=pieces_ref.at[target, shares[share]],
+                dst_ref=spread_refs[share].at[me],
+                send_sem=spread_sems.at[0, share, offset],
+                recv_sem=spread_sems.at[1, share, offset],
+                device_id={"ep": target, "sub": core},
+                device_id_type=MESH,
+            )
+            copy.start()
+            copies.append(copy)
+        own_spread = pltpu.make_async_copy(
+            pieces_ref.at[me, shares[share]], spread_refs[share].at[me], local_sem.at[2 + share]
+        )
+        own_spread.start()
+        spread_copies.append(copies + [own_spread])
 
     own_tokens.wait()
     for copy in token_copies:
@@ -335,6 +347,40 @@
             send(send_one, recv_one, one_sems, side, across_x if side == 0 else across_y)
         )
 
+    columns = pl.ds(pl.multiple_of(me * piece_columns, 128), piece_columns)
+    piece_copies = []
+
+    def move(share):
+        for copy in spread_copies[share]:
+            copy.wait()
+
+        def choose(number, carry):
+            chosen_refs[share][number] = spread_refs[share][arrive_ref[number]]
+            return carry
+
+        lax.fori_loop(0, experts, choose, 0)
+        for offset in order:
+            target = lax.rem(me + offset, experts)
+            copy = pltpu.make_async_remote_copy(
+                src_ref=chosen_refs[share].at[target],
+                dst_ref=arrived_ref.at[shares[share], columns],
+                send_sem=move_sems.at[0, share, offset],
+                recv_sem=move_sems.at[1, share, offset],
+                device_id={"ep": target, "sub": core},
+                device_id_type=MESH,
+            )
+            copy.start()
+            piece_copies.append(copy)
+        own_piece = pltpu.make_async_copy(
+            chosen_refs[share].at[me],
+            arrived_ref.at[shares[share], columns],
+            local_sem.at[4 + share],
+        )
+        own_piece.start()
+        piece_copies.append(own_piece)
+
+    move(0)
+
     two_copies = []
     for side in range(2):
         one_copies[side].wait()
@@ -362,31 +408,7 @@
             + recv_two[side, plane].astype(jnp.float32)
         )
 
-    own_spread.wait()
-    for copy in spread_copies:
-        copy.wait()
-
-    def choose(number, carry):
-        chosen_ref[number] = spread_ref[arrive_ref[number]]
-        return carry
-
-    lax.fori_loop(0, experts, choose, 0)
-    columns = pl.ds(pl.multiple_of(me * piece_columns, 128), piece_columns)
-    piece_copies = []
-    for offset in range(1, experts):
-        target = lax.rem(me + offset, experts)
-        copy = pltpu.make_async_remote_copy(
-            src_ref=chosen_ref.at[target],
-            dst_ref=arrived_ref.at[:, columns],
-            send_sem=move_sems.at[0, offset],
-            recv_sem=move_sems.at[1, offset],
-            device_id={"ep": target, "sub": core},
-            device_id_type=MESH,
-        )
-        copy.start()
-        piece_copies.append(copy)
-    own_piece = pltpu.make_async_copy(chosen_ref.at[me], arrived_ref.at[:, columns], local_sem.at[2])
-    own_piece.start()
+    move(1)
 
     for side in range(2):
         two_copies[side].wait()
@@ -414,7 +436,6 @@
         for offset in range(1, planes):
             total = total + recv_three[offset - 1, :, :, sides[side]].astype(jnp.float32)
         mixed_ref[:, :, sides[side]] = total.astype(jnp.bfloat16)
-    own_piece.wait()
     for copy in piece_copies:
         copy.wait()
     for copy in token_copies:
@@ -456,21 +477,23 @@
     blocks = half // Q_BLOCK
     planes = experts // 4
     bf16 = jnp.bfloat16
+    cuts = [half // 2, half // 2 + EXTRA_ROWS]
     mixed, arrived = pl.pallas_call(
         functools.partial(whole_kernel, experts),
         out_shape=(
             jax.ShapeDtypeStruct((steps, tokens, width), bf16),
             jax.ShapeDtypeStruct((piece_rows, width), bf16),
         ),
-        in_specs=[pl.BlockSpec(memory_space=pltpu.SMEM), vmem, any_space, vmem, vmem],
-        out_specs=(vmem, any_space),
+        in_specs=[pl.BlockSpec(memory_space=pltpu.SMEM), vmem, any_space, any_space, vmem],
+        out_specs=(vmem, vmem),
         scratch_shapes=[
             pltpu.VMEM((steps, 2, experts, tokens, half), bf16),
             pltpu.VMEM((steps, half, width), bf16),
             pltpu.VMEM((steps, max(8, blocks), width), jnp.float32),
             pltpu.VMEM((experts, piece_rows, piece_columns), bf16),
-            pltpu.VMEM((experts, piece_rows, piece_columns), bf16),
-            pltpu.VMEM((experts, piece_rows, piece_columns), bf16),
+            [pltpu.VMEM((experts, count, piece_columns), bf16) for count in cuts],
+            [pltpu.VMEM((experts, count, piece_columns), bf16) for count in cuts],
+            pltpu.VMEM((half, width), jnp.float32),
             pltpu.VMEM((steps, 2, experts, tokens, width), bf16),
             pltpu.VMEM((steps, experts, tokens, width), bf16),
             pltpu.VMEM((2, 2 * planes, steps, tokens, width // 2), bf16),
@@ -481,13 +504,13 @@
             pltpu.VMEM((planes - 1, steps, tokens, width), bf16),
             pltpu.SemaphoreType.DMA((experts, 2)),
             pltpu.SemaphoreType.DMA((experts, 2)),
-            pltpu.SemaphoreType.DMA((2, experts)),
-            pltpu.SemaphoreType.DMA((2, experts)),
+            pltpu.SemaphoreType.DMA((2, 2, experts)),
+            pltpu.SemaphoreType.DMA((2, 2, experts)),
             pltpu.SemaphoreType.DMA((2, 2)),
             pltpu.SemaphoreType.DMA((2, 2)),
             pltpu.SemaphoreType.DMA((2, 2)),
             pltpu.SemaphoreType.DMA((2, planes)),
-            pltpu.SemaphoreType.DMA((3,)),
+            pltpu.SemaphoreType.DMA((6,)),
         ],
         compiler_params=pltpu.CompilerParams(
             collective_id=0, has_side_effects=True, vmem_limit_bytes=52 * 1024 * 1024

time: 131 us -> 121 us (0.924)
  the two profiles are of different devices: /device:TPU:27 before, /device:TPU:0 now
where the time goes in v3:
time: 121 us; the launch traced here: 120 us
  Pallas kernels  108 us (89%)
  local copies, waits for them, and re-layouts  6.56 us (5%)
  other arithmetic  3.2 us (3%)
  matrix products  1.46 us (1%)
    pallas_call x1, Pallas kernels, local_small(): pl.pallas_call(functools.partial(whole_kernel, experts), out_shape=(jax.S...  108 us
    unnamed x5, local copies, waits for them, and re-layouts  3.59 us
    broadcast_in_dim x1, local copies, waits for them, and re-layouts, local_small(): return (mixed, arrived[:half][None], new_steps[None])  2.73 us

profile of v3, /device:TPU:0, one launch (start us, length us, event | category | flops | bytes accessed | tf_op | source)
XLA Modules:
  0.0 120.1 jit_solution(604668601508200843)
XLA Ops:
  0.6 1.5 %fusion.6 = (s32[]{:T(128)}, s32[16]{0:T(128)S(1)}, s32[16]{0:T(128)S(1)}, s32[16]{0:T(128)S(1)}) fusion(s32[16,4]{0,1:T(4,128)} %param.11, s32[]{:T(128)S(6)} %axis_index.15), kind=kLoop, calls=%fused_computation.25 | loop fusion | flops 47 | bytes 456 | tf_op jit(solution)/shard_map/reduce_sum | solution.py:34
  2.1 0.1 select_reduce_fusion.1
  2.2 0.7 compare_convert_fusion
  2.9 0.1 broadcast_in_dim.54.active_ref
  2.9 0.8 copy.13
  3.7 0.1 eq.81
  3.8 0.1 select_reduce_fusion
  3.9 0.8 copy.14
  4.7 0.1 mul.22
  4.8 0.8 copy.18
  5.5 1.5 %convolution_convert_fusion = bf16[512,768]{1,0:T(8,128)(2,1)S(1)} fusion(bf16[256,768]{1,0:T(8,128)(2,1)} %bitcast.20, f32[256]{0:T(256)S(1)} %mul.22, s32[256]{0:T(256)S(1)} %fusion.5), kind=kOutput, calls=%fused_computation.1 | convolution fusion | flops 202440704 | bytes 1181696 | tf_op jit(solution)/shard_map/dot_general | solution.py:474
  7.0 108.2 %shard_map.85 = (bf16[2,16,2048]{2,1,0:T(8,128)(2,1)S(1)}, bf16[400,2048]{1,0:T(8,128)(2,1)}) custom-call(s32[16]{0:T(128)S(1)} %get-tuple-element.17.arrive_ref, s32[2,128]{1,0:T(2,128)S(1)} %broadcast_in_dim.54.active_ref, bf16[16,2,16,768]{3,2,1,0:T(8,128)(2,1)S(1)} %bitcast.17, f32[384,2048]{1,0:T(8,128)} %bitcast.19, f32[3,2048]{1,0:T(4,128)S(1)} %bitcast.18), custom_call_target="tpu_custom_call" | custom-call | tf_op jit(solution)/shard_map/pallas_call | solution.py:481
  115.2 0.9 slice_convert_fusion
  116.1 2.7 %slice_bitcast_fusion = bf16[1,384,2048]{2,1,0:T(8,128)(2,1)} fusion(bf16[400,2048]{1,0:T(8,128)(2,1)} %get-tuple-element.6), kind=kLoop, calls=%fused_computation | loop fusion | bytes 3145728 | tf_op jit(solution)/shard_map/broadcast_in_dim | solution.py:521
  118.8 0.6 copy.15
  119.5 0.7 copy.20
  (2 shorter events, 0.0 us)
